TPU v7x, 256 devices: a whole 4x4x8 slice. The times are simulated.
256 devices in a mesh: expert: 16 (over z, core), mp: 16 (over y, x).
Axes of the slice: x: 4, y: 4, z: 8, core: 2. Of those that a mesh axis runs over, the one named last changes fastest.
Arguments:
- tokens: bfloat16 [4096, 8192], P('expert', 'mp'), may hold values from -6 to 6
- queries: bfloat16 [4096, 8192], P('expert', 'mp'), may hold values from -6 to 6
- attn_keys: bfloat16 [4096, 8192], P('expert', 'mp'), may hold values from -6 to 6
- router: bfloat16 [8192, 2], P('mp'), may hold values from -0.0625 to 0.0625
- w_in: bfloat16 [8192, 65536], P(None, ('expert', 'mp')), may hold values from -0.0625 to 0.0625
- w_out: bfloat16 [65536, 8192], P(('expert', 'mp')), may hold values from -0.03125 to 0.03125
- pick_rows: int32 [2, 16, 16], P(None, 'expert'), may hold values from 0 to 255, as said below
- counts: int32 [2, 16], P(None, 'expert'), may hold values from 1 to 16, 128 in all within a row
Outputs:
- expert_mixed: bfloat16 [4096, 8192], P('expert', 'mp')
- attended: bfloat16 [4096, 8192], P('expert', 'mp')
Inputs may be any that keep to these rules, and one draw needn't show every extreme that they name: `pick_rows`: for each expert and source block the 16 entries are distinct rows of that block; only the first counts entries are picks. `counts`: each expert picks 128 tokens in all.
All inputs are finite; a program needn't handle non-finite values. No bound on the sum of `counts` on one device may be relied on, other than what follows from the above.
Results may differ from a plain program's by a relative error of at most 0.0059.
Values may be sent and summed in bfloat16 or wider, within the bound.
A program may use at most 128 MiB of HBM per device.

v0:
```python
import jax
import jax.numpy as jnp
from jax import lax
from jax.sharding import PartitionSpec as P

HEAD_DIM = 128


def body(tokens, queries, attn_keys, router, w_in, w_out, pick_rows, counts):
    tok_dev, width_part = tokens.shape
    expert_devs = lax.axis_size("expert")
    experts_here = counts.shape[0]
    group_size = expert_devs // experts_here
    slot_count = pick_rows.shape[2]
    my_picks = pick_rows[:, 0, :]
    my_counts = counts[:, 0]
    live_slots = jnp.arange(slot_count, dtype=jnp.int32)[None, :] < my_counts[:, None]
    partial_logits = jnp.dot(tokens, router, preferred_element_type=jnp.float32)
    logits = lax.psum(partial_logits, "mp")
    picked = jnp.where(live_slots[:, :, None], tokens[my_picks], 0)
    outgoing = jnp.repeat(picked, group_size, axis=0)
    arrived = lax.all_to_all(outgoing, "expert", split_axis=0, concat_axis=0, tiled=True)
    picked_rows = arrived.reshape(expert_devs * slot_count, width_part)
    weight_part = w_in
    preact = jnp.dot(
        lax.all_gather(picked_rows, "mp", axis=1, tiled=True),
        weight_part,
        preferred_element_type=jnp.float32,
    )
    hidden_t = jax.nn.gelu(preact).astype(jnp.bfloat16).T
    weight_part = w_out
    out_t = lax.psum_scatter(
        lax.dot_general(
            weight_part, hidden_t, (((0,), (0,)), ((), ())), preferred_element_type=jnp.float32
        ).astype(jnp.bfloat16),
        "mp",
        scatter_dimension=0,
        tiled=True,
    ).astype(jnp.float32)
    returned = lax.all_to_all(
        out_t.reshape(width_part, expert_devs, slot_count).astype(jnp.bfloat16),
        "expert",
        split_axis=1,
        concat_axis=1,
        tiled=True,
    ).astype(jnp.float32)
    contrib = returned.reshape(width_part, experts_here, group_size, slot_count).sum(axis=2)
    gate_value = jax.nn.sigmoid(jnp.take_along_axis(logits.T, my_picks, axis=1))
    slot_scale = jnp.where(live_slots, gate_value, 0.0)
    weighted = (contrib * slot_scale[None]).reshape(width_part, experts_here * slot_count).T
    update = jnp.zeros((tok_dev, width_part), jnp.float32).at[my_picks.reshape(-1)].add(weighted)
    expert_mixed = (tokens.astype(jnp.float32) + update).astype(jnp.bfloat16)
    heads_here = width_part // HEAD_DIM
    inv_root = HEAD_DIM ** (-0.5)
    query_heads = queries.reshape(tok_dev, heads_here, HEAD_DIM)
    first_row = lax.axis_index("expert") * tok_dev
    query_pos = first_row + jnp.arange(tok_dev, dtype=jnp.int32)
    key_part = lax.all_gather(attn_keys, "expert", axis=0, tiled=True)
    value_part = lax.all_gather(expert_mixed, "expert", axis=0, tiled=True)
    length = key_part.shape[0]
    key_heads = key_part.reshape(length, heads_here, HEAD_DIM)
    value_heads = value_part.reshape(length, heads_here, HEAD_DIM)
    running_max = jnp.full((heads_here, tok_dev), -1e30, jnp.float32)
    scores = (
        jnp.einsum("qhd,khd->hqk", query_heads, key_heads, preferred_element_type=jnp.float32)
        * inv_root
    )
    allowed = jnp.arange(length, dtype=jnp.int32)[None, :] <= query_pos[:, None]
    block_max = jnp.max(jnp.where(allowed[None], scores, -1e30), axis=2)
    new_max = jnp.maximum(running_max, block_max)
    weights = jnp.where(allowed[None], jnp.exp(scores - new_max[..., None]), 0.0)
    denominator = jnp.sum(weights, axis=2)
    numerator = jnp.einsum(
        "hqk,khd->hqd",
        weights.astype(jnp.bfloat16),
        value_heads,
        preferred_element_type=jnp.float32,
    )
    final_max, denominator, numerator = (new_max, denominator, numerator)
    attended = (
        (numerator / denominator[..., None])
        .transpose(1, 0, 2)
        .reshape(tok_dev, width_part)
        .astype(jnp.bfloat16)
    )
    return (expert_mixed, attended)


def solution(mesh):
    placed = (
        P("expert", "mp"),
        P("expert", "mp"),
        P("expert", "mp"),
        P("mp", None),
        P(None, ("expert", "mp")),
        P(("expert", "mp"), None),
        P(None, "expert", None),
        P(None, "expert"),
    )
    return jax.shard_map(
        body,
        mesh=mesh,
        in_specs=placed,
        out_specs=(P("expert", "mp"), P("expert", "mp")),
        check_vma=False,
    )
```

profile of v0, /device:TPU:1, one launch (start us, length us, event | category | flops | bytes accessed | tf_op | source)
XLA Modules:
  0.0 299.4 jit_solution(17805244128195197436)
XLA Ops:
  8.0 0.0 copy-start
  8.0 0.0 all-gather.4.cloned.1.call-start
  8.1 0.8 iota_compare_fusion.1
  8.8 0.7 shift-left_or_fusion
  9.5 0.1 reshape.202
  9.6 1.6 gather_fusion
  11.2 0.1 broadcast_select_fusion
  11.3 21.6 %all_to_all.10 = bf16[16,16,512]{2,1,0:T(8,128)(2,1)} all-to-all(bf16[16,16,512]{2,1,0:T(8,128)(2,1)S(1)} %bitcast.54), channel_id=1, replica_groups=mesh['expert'=16,'mp'=16] {'expert'}, dimensions={0} | all-to-all | bytes 524288 | tf_op jit(solution)/shard_map/all_to_all | solution.py:22
  32.9 0.0 all-gather.4.cloned.1.call-update
  32.9 0.0 reduce-scatter.2.cloned.1.call-start
  33.0 58.5 %all-gather.4.cloned.1.call-done = bf16[256,8192]{1,0:T(8,128)(2,1)} async-done(((bf16[256,512]{1,0:T(8,128)(2,1)}), bf16[256,8192]{1,0:T(8,128)(2,1)}) %all-gather.4.cloned.1.call-update) | async-done | bytes 4194320 | tf_op jit(solution)/shard_map/all_gather | solution.py:26
  91.5 11.2 %fusion.2 = bf16[8192,256]{0,1:T(8,128)(2,1)} fusion(bf16[256,8192]{1,0:T(8,128)(2,1)} %param.13, bf16[256,8192]{1,0:T(8,128)(2,1)} %all-gather.4.cloned.1.call-done, bf16[8192,256]{1,0:T(8,128)(2,1)} %param.12), kind=kOutput, calls=%fused_computation.8 | convolution fusion | flops 2150170624 | bytes 16777216 | tf_op jit(solution)/shard_map/dot_general | solution.py:33
  102.7 0.0 copy-start.6
  102.7 0.0 reduce-scatter.2.cloned.1.call-update
  102.8 0.0 all-gather.6.cloned.1.call-start
  102.8 0.8 copy-done.3
  103.7 0.8 copy.13
  104.5 0.0 all-gather.6.cloned.1.call-update
  104.5 79.9 %reduce-scatter.2.cloned.1.call-done = bf16[512,256]{0,1:T(8,128)(2,1)} async-done(((bf16[8192,256]{0,1:T(8,128)(2,1)}), bf16[512,256]{0,1:T(8,128)(2,1)}) %reduce-scatter.2.cloned.1.call-update) | async-done | bytes 262160 | tf_op jit(solution)/shard_map/reduce_scatter | solution.py:32
  184.4 9.4 %all-to-all-start.1 = ((bf16[512,16,16]{0,2,1:T(8,128)(2,1)}), bf16[512,16,16]{0,2,1:T(8,128)(2,1)S(1)}, u32[]{:S(2)}, u32[]{:S(2)}) async-start(bf16[512,16,16]{0,2,1:T(8,128)(2,1)} %bitcast.55), calls=%async_computation.2 | async-start | bytes 524288 | tf_op jit(solution)/shard_map/all_to_all | solution.py:40
  193.8 0.0 all-gather.8.cloned.1.call-start
  193.8 0.0 copy-done.2
  193.8 0.1 fusion.42
  194.0 0.1 convert_element_type.32
  194.1 0.1 squeeze.6
  194.2 0.5 broadcast.146
  194.7 0.7 reduce.5
  195.3 0.1 reshape_squeeze.3
  195.4 0.1 lt.80
  195.5 0.1 lt.81
  195.6 0.1 lt.79
  195.7 0.1 reshape.208
  195.7 30.9 %psum.7 = f32[2,256]{1,0:T(2,128)S(1)} all-reduce(f32[2,256]{1,0:T(2,128)S(1)} %fusion.42), channel_id=1, replica_groups=mesh['expert'=16,'mp'=16] {'mp'}, use_global_device_ids=true, to_apply=%region_2.3 | all-reduce | flops 512 | bytes 4096 | tf_op jit(solution)/shard_map/psum | solution.py:19
  226.7 0.8 gather_fusion.1
  227.5 0.0 all-to-all-done.1
  227.5 0.1 bitcast_multiply_fusion
  227.6 1.0 scatter_custom_fusion
  228.6 0.7 convert_element_type.37
  229.3 0.0 all-gather.8.cloned.1.call-update
  229.4 0.7 iota_compare_fusion
  230.1 0.0 all-gather.6.cloned.1.call-done
  230.1 5.4 %select_reduce_fusion = (f32[4,256]{1,0:T(4,128)S(1)}, f32[4,256,4096]{2,1,0:T(8,128)S(1)}) fusion(pred[256,4096]{1,0:T(8,128)(4,1)S(1)} %iota_compare_fusion, bf16[4096,4,128]{0,2,1:T(8,128)(2,1)} %bitcast.51, bf16[256,512]{1,0:T(8,128)(2,1)S(1)} %copy-done), kind=kOutput, calls=%fused_computation.4 | convolution fusion | flops 1086323712 | bytes 22286336 | tf_op jit(solution)/shard_map/qhd,khd->hqk/dot_general | solution.py:65
  235.5 5.7 %copy-done.1 = f32[4,256,4096]{2,1,0:T(8,128)} copy-done((f32[4,256,4096]{2,1,0:T(8,128)}, f32[4,256,4096]{2,1,0:T(8,128)S(1)}, u32[]{:S(2)}) %copy-start.1) | copy-done | bytes 16777240
  241.2 4.5 %fusion = f32[4,256]{1,0:T(4,128)S(1)} fusion(f32[4,256,4096]{2,1,0:T(8,128)S(1)} %get-tuple-element.9, f32[4,256]{1,0:T(4,128)S(1)} %broadcast_maximum_fusion, pred[256,4096]{1,0:T(8,128)(4,1)S(1)} %iota_compare_fusion), kind=kLoop, calls=%fused_computation.5 | loop fusion | flops 16776192 | bytes 17833984 | tf_op jit(solution)/shard_map/reduce_sum | solution.py:72
  245.7 29.7 %all-gather.8.cloned.1.call-done = bf16[4096,512]{1,0:T(8,128)(2,1)} async-done(((bf16[256,512]{1,0:T(8,128)(2,1)}), bf16[4096,512]{1,0:T(8,128)(2,1)}) %all-gather.8.cloned.1.call-update) | async-done | bytes 4194320 | tf_op jit(solution)/shard_map/all_gather | solution.py:59
  275.5 6.5 %copy.16 = bf16[4096,512]{0,1:T(8,128)(2,1)} copy(bf16[4096,512]{1,0:T(8,128)(2,1)} %all-gather.8.cloned.1.call-done) | data formatting | bytes 8388608 | tf_op jit(solution)/shard_map/all_gather | solution.py:59
  282.0 9.1 %fusion.12 = bf16[256,4,128]{0,2,1:T(8,128)(2,1)S(1)} fusion(bf16[4096,4,128]{0,2,1:T(8,128)(2,1)} %bitcast.52, f32[4,256,4096]{2,1,0:T(8,128)} %copy-done.1, f32[4,256]{1,0:T(4,128)S(1)} %broadcast_maximum_fusion, pred[256,4096]{1,0:T(8,128)(4,1)S(1)} %iota_compare_fusion, f32[256,4]{0,1:T(4,128)S(1)} %bitcast.60), kind=kOutput, calls=%fused_computation.14 | convolution fusion | flops 1090781184 | bytes 22290432 | tf_op jit(solution)/shard_map/hqk,khd->hqd/dot_general | solution.py:73
  291.1 0.8 copy.17
  (17 shorter events, 0.1 us)
Async XLA Ops:
  8.0 222.1 %copy-start = (bf16[256,512]{1,0:T(8,128)(2,1)S(1)}, bf16[256,512]{1,0:T(8,128)(2,1)}, u32[]{:S(2)}) copy-start(bf16[256,512]{1,0:T(8,128)(2,1)} %param.9) | copy-start | bytes 786436
  8.0 83.5 %all-gather.4.cloned.1.call-start = ((), (), s32[]{:S(2)}) async-start(), calls=%async_computation.3 | async-start | bytes 4456448 | tf_op jit(solution)/shard_map/all_gather | solution.py:26
  32.9 151.4 %reduce-scatter.2.cloned.1.call-start = ((), (), s32[]{:S(2)}) async-start(), calls=%async_computation.4 | async-start | bytes 4456448 | tf_op jit(solution)/shard_map/reduce_scatter | solution.py:32
  102.7 0.9 copy-start.3
  102.7 91.1 %copy-start.2 = (bf16[256,512]{1,0:T(8,128)(2,1)S(1)}, bf16[256,512]{1,0:T(8,128)(2,1)}, u32[]{:S(2)}) copy-start(bf16[256,512]{1,0:T(8,128)(2,1)} %param.8) | copy-start | bytes 786436
  102.7 91.1 %copy-start.5 = (bf16[512,2]{0,1:T(2,128)(2,1)S(1)}, bf16[512,2]{0,1:T(2,128)(2,1)}, u32[]{:S(2)}) copy-start(bf16[512,2]{0,1:T(2,128)(2,1)} %param.11) | copy-start | bytes 6148
  102.7 91.4 %copy-start.4 = (s32[2,1,16]{2,1,0:T(1,128)S(1)}, s32[2,1,16]{2,1,0:T(1,128)}, u32[]{:S(2)}) copy-start(s32[2,1,16]{2,1,0:T(1,128)} %param.14) | copy-start | bytes 388
  102.7 92.7 %copy-start.6 = (s32[2,1]{0,1:T(1,128)S(1)}, s32[2,1]{0,1:T(1,128)}, u32[]{:S(2)}) copy-start(s32[2,1]{0,1:T(1,128)} %param.15) | copy-start | bytes 28
  102.8 127.3 %all-gather.6.cloned.1.call-start = ((), (), s32[]{:S(2)}) async-start(), calls=%async_computation.5 | async-start | bytes 4456448 | tf_op jit(solution)/shard_map/all_gather | solution.py:58
  184.4 43.1 %all-to-all-start.1 = ((bf16[512,16,16]{0,2,1:T(8,128)(2,1)}), bf16[512,16,16]{0,2,1:T(8,128)(2,1)S(1)}, u32[]{:S(2)}, u32[]{:S(2)}) async-start(bf16[512,16,16]{0,2,1:T(8,128)(2,1)} %bitcast.55), calls=%async_computation.2 | async-start | bytes 524288 | tf_op jit(solution)/shard_map/all_to_all | solution.py:40
  193.8 81.7 %all-gather.8.cloned.1.call-start = ((), (), s32[]{:S(2)}) async-start(), calls=%async_computation.6 | async-start | bytes 4456448 | tf_op jit(solution)/shard_map/all_gather | solution.py:59
  235.5 5.7 %copy-start.1 = (f32[4,256,4096]{2,1,0:T(8,128)}, f32[4,256,4096]{2,1,0:T(8,128)S(1)}, u32[]{:S(2)}) copy-start(f32[4,256,4096]{2,1,0:T(8,128)S(1)} %get-tuple-element.9) | copy-start | bytes 50331652
Sparse Core Ops, SparseCore 0:
  33.1 58.4 all-gather.3
  102.9 81.4 reduce-scatter.1
Sparse Core Ops, SparseCore 1:
  105.7 49.9 all-gather.5
  229.5 46.0 all-gather.7
where the time goes:
time: 300 us; the launch traced here: 299 us
  waiting for transfers between devices  168 us (56%)
  blocking collectives  52.5 us (18%)
  matrix products  25.9 us (9%)
  local copies, waits for them, and re-layouts  18.2 us (6%)
  between operations  15.7 us (5%)
  starting transfers between devices  9.54 us (3%)
  other arithmetic  9.33 us (3%)
    reduce_scatter x1, waiting for transfers between devices, body(): lax.psum_scatter(lax.dot_general(weight_part, hidden_t, (((0,), (0,)), ((...  79.9 us
    all_gather x1, waiting for transfers between devices, body(): lax.all_gather(picked_rows, 'mp', axis=1, tiled=True)  58.5 us
    psum x1, blocking collectives, body(): logits = lax.psum(partial_logits, 'mp')  30.9 us
    all_gather x1, waiting for transfers between devices, body(): value_part = lax.all_gather(expert_mixed, 'expert', axis=0, tiled=True)  29.7 us
    all_to_all x1, blocking collectives, body(): lax.all_to_all(outgoing, 'expert', split_axis=0, concat_axis=0, tiled=True)  21.6 us
    dot_general x1, matrix products, body(): lax.dot_general(weight_part, hidden_t, (((0,), (0,)), ((), ())), preferre...  11.2 us
    all_to_all x1, starting transfers between devices, body(): lax.all_to_all(out_t.reshape(width_part, expert_devs, slot_count).astype(...  9.38 us
    dot_general x1, matrix products, body(): jnp.einsum('hqk,khd->hqd', weights.astype(jnp.bfloat16), value_heads, pre...  9.14 us
  transfers between devices with their start and end apart: 5, of which 3 were waited for; matrix products, arithmetic and copies ran while one was open for 5% of the time, Pallas kernels for 0%

commit v1 on v0

v1 whole, which is shorter than its diff:
```python
import jax
import jax.numpy as jnp
from jax import lax
from jax.experimental import pallas as pl
from jax.experimental.pallas import tpu as pltpu
from jax.sharding import PartitionSpec as P

MESH = pl.DeviceIdType.MESH
HEAD_DIM = 128
BF = jnp.bfloat16
F32 = jnp.float32
NT = (((1,), (1,)), ((), ()))
INV_ROOT = HEAD_DIM ** (-0.5)
CUT, BLOCK_ROWS = 80, 144


def dot(a, b):
    return jnp.dot(a, b, preferred_element_type=F32)


def dot_nt(a, b):
    return lax.dot_general(a, b, NT, preferred_element_type=F32)


def kernel(
    tok, qry, key, rt, win, wout, picks, cnts, mixed_o, att_o,
    a_msg, a_buf, xg, w1, w2, part, part_in, lgacc, hid, gate_s,
    outb, t_own, rs_h, rs_f, t_sum, rp_h, rp_f, e_buf, u_buf,
    kb, vb, acc, mrow, lrow, kp, wp, pos_col, pos_row,
    loc_sem, a_ss, a_rs, w_ss, w_rs, g_ss, g_rs, x_ss, x_rs,
    r_ss, r_rs, e_ss, e_rs, ep_ss, ep_rs, kv_ss, kv_rs, kvp_ss, kvp_rs,
):
    e = lax.axis_index("expert")
    m = lax.axis_index("mp")
    z, c = e // 2, lax.rem(e, 2)
    y, x = m // 4, lax.rem(m, 4)
    oc = 1 - c
    group = z // 4

    def dev(dz=0, dc=0, dy=0, dx=0):
        zz = lax.rem(z + dz + 8, 8)
        cc = lax.rem(c + dc, 2)
        return (zz * 2 + cc, lax.rem(y + dy + 4, 4) * 4 + lax.rem(x + dx + 4, 4))

    def along(i, j):
        return c * i + oc * j, oc * i + c * j

    def blk(i, j):
        dy, dx = along(i, j)
        return lax.rem(y + dy + 4, 4) * 4 + lax.rem(x + dx + 4, 4)

    def pdev(d):
        dy, dx = along(d, 0)
        return dev(dy=dy, dx=dx)

    def sdev(d):
        dy, dx = along(0, d)
        return dev(dy=dy, dx=dx)

    partner = dev(dc=1)
    sent = []

    def send(src, dst, ss, rs, to):
        cp = pltpu.make_async_remote_copy(
            src_ref=src, dst_ref=dst, send_sem=ss, recv_sem=rs, device_id=to, device_id_type=MESH
        )
        cp.start()
        sent.append(cp)
        return cp

    w1_loc = pltpu.make_async_copy(win.at[:, c], w1.at[c], loc_sem.at[0])
    w1_loc.start()
    barrier = pltpu.get_barrier_semaphore()
    for dz in range(8):
        for dc in range(2):
            if dz or dc:
                pl.semaphore_signal(barrier, inc=1, device_id=dev(dz, dc), device_id_type=MESH)
    for d in (1, -1):
        pl.semaphore_signal(barrier, inc=1, device_id=dev(dy=d), device_id_type=MESH)
        pl.semaphore_signal(barrier, inc=1, device_id=dev(dx=d), device_id_type=MESH)

    row32 = lax.broadcasted_iota(jnp.int32, (32, 256), 0)
    lane32 = lax.broadcasted_iota(jnp.int32, (32, 256), 1)
    chosen = jnp.full((32, 256), -1, jnp.int32)
    row16 = lax.broadcasted_iota(jnp.int32, (16, 128), 0)
    lane16 = lax.broadcasted_iota(jnp.int32, (16, 128), 1)
    meta = jnp.where(row16 == 0, cnts[0, 0], jnp.where(row16 == 1, cnts[1, 0], 0))
    base = 16 * lax.rem(e, 8)
    for g in range(2):
        for j in range(16):
            pick = picks[g, 0, j]
            live = jnp.where(j < cnts[g, 0], pick, -1)
            chosen = jnp.where(row32 == 16 * g + j, live, chosen)
            meta = jnp.where(
                (row16 == 2 + 2 * g + e // 8) & (lane16 == base + j), pick, meta
            )
    onehot = jnp.where(chosen == lane32, 1.0, 0.0).astype(BF)
    rows = dot(onehot, tok[...]).astype(BF)
    meta_b = meta.astype(F32).astype(BF)
    for g in range(2):
        for h in range(2):
            a_msg[g, h, 0:16, :] = rows[16 * g : 16 * g + 16, 256 * h : 256 * h + 128]
            a_msg[g, h, 16:32, :] = rows[16 * g : 16 * g + 16, 256 * h + 128 : 256 * h + 256]
            a_msg[g, h, 32:48, :] = meta_b
    a_buf[e] = a_msg[group, c]
    pl.semaphore_wait(barrier, 19)

    a_cps = []
    for dz in (4, 3, 5, 2, 6, 1, 7, 0):
        for dc in range(2):
            if dz or dc:
                to_plane = lax.rem(z + dz, 8)
                to_core = lax.rem(c + dc, 2)
                a_cps.append(
                    send(
                        a_msg.at[to_plane // 4, to_core], a_buf.at[e],
                        a_ss.at[dz * 2 + dc], a_rs.at[dz * 2 + dc], dev(dz, dc),
                    )
                )

    def kv_send(buf, which, r_from, r_to, way, src=None):
        src = buf.at[r_from, c] if src is None else src
        return send(
            src, buf.at[r_to, c], kv_ss.at[which, r_to, way], kv_rs.at[which, r_to, way],
            dev(dz=1 if way == 0 else -1),
        )

    def kv_share(buf, which, r, src=None):
        src = buf.at[r, c] if src is None else src
        return send(src, buf.at[r, c], kvp_ss.at[which, r], kvp_rs.at[which, r], partner)

    pieces = {}
    shared = {}
    pieces["k", 1] = kv_send(kb, 0, 0, 1, 0, key)
    pieces["v", 7] = kv_send(vb, 1, 0, 7, 1, tok)
    shared["k", 0] = kv_share(kb, 0, 0, key)
    shared["v", 0] = kv_share(vb, 1, 0, tok)
    pieces["v", 1] = kv_send(vb, 1, 0, 1, 0, tok)
    pieces["k", 7] = kv_send(kb, 0, 0, 7, 1, key)
    right = [("k", 1), ("v", 1), ("k", 2), ("v", 2), ("k", 3), ("v", 3), ("k", 4)]
    left = [("v", 7), ("k", 7), ("v", 6), ("k", 6), ("v", 5), ("k", 5), ("v", 4)]

    def pump(n):
        for way, (what, r) in ((0, right[n]), (1, left[n])):
            pieces[what, r].wait_recv()
            which, buf = (0, kb) if what == "k" else (1, vb)
            r_to = r + 1 if way == 0 else r - 1
            if (what, r_to) in (right if way == 0 else left):
                pieces[what, r_to] = kv_send(buf, which, r, r_to, way)
            shared[what, r] = kv_share(buf, which, r)

    w1_far = send(win.at[:, oc], w1.at[c], w_ss.at[0], w_rs.at[0], partner)

    def w2_copies():
        for b in range(16):
            mine = pl.ds(pl.multiple_of(512 * b + 256 * c, 256), 256)
            pltpu.make_async_copy(wout.at[:, mine], w2.at[c, b], loc_sem.at[1]).start()
        for b in range(16):
            other = pl.ds(pl.multiple_of(512 * b + 256 * oc, 256), 256)
            pltpu.make_async_remote_copy(
                src_ref=wout.at[:, other], dst_ref=w2.at[c, b], send_sem=w_ss.at[1],
                recv_sem=w_rs.at[1], device_id=partner, device_id_type=MESH,
            ).start()

    w2_copies()
    w2_loc = pltpu.make_async_copy(w2.at[c], w2.at[c], loc_sem.at[1])
    w2_far = pltpu.make_async_remote_copy(
        src_ref=w2.at[c], dst_ref=w2.at[c], send_sem=w_ss.at[1], recv_sem=w_rs.at[1],
        device_id=partner, device_id_type=MESH,
    )

    def soft_step(h, scores, v_h):
        hs = pl.ds(pl.multiple_of(h * 128, 128), 128)
        old = mrow[h][:, 0:1]
        new = jnp.maximum(old, jnp.max(scores, axis=1, keepdims=True))
        alpha = jnp.exp((old - new) * INV_ROOT)
        w = jnp.exp((scores - new) * INV_ROOT)
        total = w[:, 0:128]
        for i in range(1, scores.shape[1] // 128):
            total = total + w[:, 128 * i : 128 * i + 128]
        lrow[h] = lrow[h] * alpha + total
        acc[:, hs] = acc[:, hs] * alpha + dot(w.astype(BF), v_h)
        mrow[h] = jnp.broadcast_to(new, (256, 128))

    def attend_own():
        allowed = lax.broadcasted_iota(jnp.int32, (256, 256), 1) <= lax.broadcasted_iota(
            jnp.int32, (256, 256), 0
        )

        @pl.loop(0, 4)
        def _(h):
            hs = pl.ds(pl.multiple_of(h * 128, 128), 128)
            scores = jnp.where(allowed, dot_nt(qry[:, hs], key[:, hs]), -1e30)
            new = jnp.max(scores, axis=1, keepdims=True)
            w = jnp.exp((scores - new) * INV_ROOT)
            lrow[h] = w[:, 0:128] + w[:, 128:256]
            acc[:, hs] = dot(w.astype(BF), tok[:, hs])
            mrow[h] = jnp.broadcast_to(new, (256, 128))

    def attend_partner():
        @pl.loop(0, 4)
        def _(h):
            hs = pl.ds(pl.multiple_of(h * 128, 128), 128)
            soft_step(h, dot_nt(qry[:, hs], kb[0, 0, :, hs]), vb[0, 0, :, hs])

    def attend_chip(r):
        @pl.loop(0, 4)
        def _(h):
            hs = pl.ds(pl.multiple_of(h * 128, 128), 128)
            k_h = kb[r, :, :, hs].reshape(512, 128)
            v_h = vb[r, :, :, hs].reshape(512, 128)
            soft_step(h, dot_nt(qry[:, hs], k_h), v_h)

    def pick_keys(first, k_rows):
        n = k_rows.shape[0]
        at = lax.broadcasted_iota(jnp.int32, (256, n), 1) + first
        sel = jnp.where(pos_col[:, 0:1] == at, 1.0, 0.0).astype(BF)
        kp[...] += dot(sel, k_rows)

    def attend_far(d):
        for r, ok in ((d, z >= d), (8 - d, z >= 8 - d)):
            for what in ("k", "v"):
                shared[what, r].wait_recv()

            @pl.when(ok)
            def _():
                attend_chip(r)
                pick_keys((z - r) * 512, kb[r].reshape(512, 512))

            if d == 4:
                break

    attend_own()
    for what in ("k", "v"):
        shared[what, 0].wait_recv()

    @pl.when(c == 1)
    def _():
        attend_partner()

    for cp in a_cps:
        cp.wait_recv()
    lane_f = lane16.astype(F32)
    run = jnp.zeros((16, 128), F32)
    slot_at = [jnp.full((16, 128), -1.0, F32), jnp.full((16, 128), -1.0, F32)]
    picked_lane = jnp.zeros((16, 128), F32)
    for s in range(16):
        t = a_buf[s, 32:48, :].astype(F32)
        j = lane_f - 16.0 * (s % 8)
        here = (lane16 // 16 == s % 8) & (j < t)
        slot_at[s // 8] = jnp.where(here, run + j, slot_at[s // 8])
        run = run + t
        picked_lane = picked_lane + t
    row_f = lax.broadcasted_iota(jnp.int32, (128, 256), 0).astype(F32)
    row_l = lax.broadcasted_iota(jnp.int32, (16, 256), 0)
    lane_l = lax.broadcasted_iota(jnp.int32, (16, 256), 1)
    compact = []
    for g in range(2):
        at = jnp.concatenate([slot_at[0][g : g + 1], slot_at[1][g : g + 1]], axis=1)
        cmat = jnp.where(row_f == at, 1.0, 0.0).astype(BF)
        compact.append(cmat)
    mine = jnp.where(group == 0, compact[0].astype(F32), compact[1].astype(F32)).astype(BF)
    for h in range(2):
        got = a_buf[:, 16 * h : 16 * h + 16, :].reshape(256, 128)
        xg[m, 0:128, 128 * h : 128 * h + 128] = dot(mine, got).astype(BF)
    half_lanes = pl.ds(pl.multiple_of(256 * c, 256), 256)
    xg[m, 128:144, :] = rt[group, :, half_lanes]

    g_cps = {}

    def g_send(idx, b, lo, hi, to):
        g_cps[idx] = send(
            xg.at[b, pl.ds(lo, hi - lo)], xg.at[b, pl.ds(lo, hi - lo)],
            g_ss.at[idx], g_rs.at[idx], to,
        )

    def g_second(i):
        g_send(4 + 4 * i, blk(i, 0), 0, BLOCK_ROWS, sdev(1))
        g_send(5 + 4 * i, blk(i, 0), 0, BLOCK_ROWS, sdev(-1))

    def g_second_half(i):
        g_cps[4 + 4 * i].wait_recv()
        g_send(6 + 4 * i, blk(i, 3), 0, CUT, sdev(1))
        g_cps[5 + 4 * i].wait_recv()
        g_send(7 + 4 * i, blk(i, 1), CUT, BLOCK_ROWS, sdev(-1))

    g_send(0, m, 0, BLOCK_ROWS, pdev(1))
    g_send(1, m, 0, BLOCK_ROWS, pdev(-1))
    g_second(0)

    at_lane = []
    for g in range(2):
        pk = jnp.concatenate(
            [picked_lane[2 + 2 * g : 3 + 2 * g], picked_lane[3 + 2 * g : 4 + 2 * g]], axis=1
        )
        info = jnp.where(
            row_l == 0, jnp.broadcast_to(pk, (16, 256)), (lane_l // 16).astype(F32)
        ).astype(BF)
        col = dot_nt(compact[g], info)
        pos_col[128 * g : 128 * g + 128, :] = jnp.broadcast_to(
            (col[:, 0:1] + 256.0 * col[:, 1:2]).astype(jnp.int32), (128, 128)
        )
        lane = dot_nt(info, compact[g])
        at_lane.append((lane[0:1] + 256.0 * lane[1:2]).astype(jnp.int32))
    pos_row[...] = jnp.broadcast_to(jnp.concatenate(at_lane, axis=1), (8, 256))
    kp[...] = jnp.zeros((256, 512), F32)
    pick_keys(e * 256, key[...])

    @pl.when(c == 1)
    def _():
        pick_keys(z * 512, kb[0, 0])

    pump(0)
    part[...] = jnp.zeros((128, 640), F32)
    lgacc[...] = jnp.zeros((128, 16), F32)
    w1_loc.wait()
    w1_far.wait_recv()

    def mm1(i, j):
        b = blk(i, j)
        xb = xg[b, 0:128, :]
        part[:, 0:256] += dot(xb, w1[0, b])
        part[:, 256:512] += dot(xb, w1[1, b])
        lgacc[...] += dot_nt(xb, xg[b, 128:144, :])

    mm1(0, 0)
    g_cps[0].wait_recv()
    g_send(2, blk(3, 0), 0, CUT, pdev(1))
    g_second(3)
    g_cps[1].wait_recv()
    g_send(3, blk(1, 0), CUT, BLOCK_ROWS, pdev(-1))
    g_second(1)
    mm1(3, 0)
    mm1(1, 0)
    g_second_half(0)
    mm1(0, 3)
    mm1(0, 1)
    g_cps[2].wait_recv()
    g_cps[3].wait_recv()
    g_second(2)
    mm1(2, 0)
    pump(1)
    for i in (3, 1, 2):
        g_second_half(i)
        mm1(i, 3)
        mm1(i, 1)
    attend_far(1)
    pump(2)
    for i in (0, 3, 1, 2):
        g_cps[6 + 4 * i].wait_recv()
        g_cps[7 + 4 * i].wait_recv()
        mm1(i, 2)

    part[:, 512:640] = jnp.broadcast_to(lgacc[:, 0:1], (128, 128))
    x_cp = send(part, part_in, x_ss.at[0], x_rs.at[0], partner)
    w2_loc.wait()
    w2_far.wait_recv()
    x_cp.wait_recv()
    hid[...] = jax.nn.gelu(part[:, 0:512] + part_in[:, 0:512]).astype(BF)
    gate_s[...] = jax.nn.sigmoid(part[:, 512:640] + part_in[:, 512:640])

    def mm2(i, j):
        b = blk(i, j)
        o = dot(hid[:, 0:256], w2[0, b]) + dot(hid[:, 256:512], w2[1, b])
        return o * gate_s[:, 0:1]

    r_cps = {}

    def r_send(idx, src, dst, to):
        r_cps[idx] = send(src, dst, r_ss.at[idx], r_rs.at[idx], to)

    order = (2, 3, 1, 0)
    for i in order:
        outb[i, 2] = mm2(i, 2).astype(BF)
        r_send(4 * i, outb.at[i, 2, pl.ds(0, 64)], rs_h.at[i, 0], sdev(1))
        r_send(4 * i + 1, outb.at[i, 2, pl.ds(64, 64)], rs_h.at[i, 1], sdev(-1))
    for i in order:
        o1 = mm2(i, 1)
        o3 = mm2(i, 3)
        r_cps[4 * i].wait_recv()
        outb[i, 1, 0:64] = (o1[0:64] + rs_h[i, 0].astype(F32)).astype(BF)
        outb[i, 1, 64:128] = o1[64:128].astype(BF)
        r_send(4 * i + 2, outb.at[i, 1], rs_f.at[i, 0], sdev(1))
        r_cps[4 * i + 1].wait_recv()
        outb[i, 3, 0:64] = o3[0:64].astype(BF)
        outb[i, 3, 64:128] = (o3[64:128] + rs_h[i, 1].astype(F32)).astype(BF)
        r_send(4 * i + 3, outb.at[i, 3], rs_f.at[i, 1], sdev(-1))
        t_own[i] = mm2(i, 0)
    pump(3)

    def t_of(i):
        r_cps[4 * i + 2].wait_recv()
        r_cps[4 * i + 3].wait_recv()
        return t_own[i] + rs_f[i, 0].astype(F32) + rs_f[i, 1].astype(F32)

    t_sum[2] = t_of(2).astype(BF)
    r_send(16, t_sum.at[2, pl.ds(0, 64)], rp_h.at[0], pdev(1))
    r_send(17, t_sum.at[2, pl.ds(64, 64)], rp_h.at[1], pdev(-1))
    t3 = t_of(3)
    t1 = t_of(1)
    r_cps[17].wait_recv()
    t_sum[3, 0:64] = t3[0:64].astype(BF)
    t_sum[3, 64:128] = (t3[64:128] + rp_h[1].astype(F32)).astype(BF)
    r_send(18, t_sum.at[3], rp_f.at[1], pdev(-1))
    r_cps[16].wait_recv()
    t_sum[1, 0:64] = (t1[0:64] + rp_h[0].astype(F32)).astype(BF)
    t_sum[1, 64:128] = t1[64:128].astype(BF)
    r_send(19, t_sum.at[1], rp_f.at[0], pdev(1))
    attend_far(2)
    pump(4)
    t0 = t_of(0)
    r_cps[18].wait_recv()
    r_cps[19].wait_recv()
    e_buf[0, c] = (t0 + rp_f[0].astype(F32) + rp_f[1].astype(F32)).astype(BF)

    e_cps = {}
    ep_cps = {}

    def e_send(r_from, r_to, way, lo, hi):
        e_cps[r_to, way] = send(
            e_buf.at[r_from, c, pl.ds(lo, hi - lo)], e_buf.at[r_to, c, pl.ds(lo, hi - lo)],
            e_ss.at[r_to, way], e_rs.at[r_to, way], dev(dz=1 if way == 0 else -1),
        )

    def e_share(r):
        ep_cps[r] = send(e_buf.at[r, c], e_buf.at[r, c], ep_ss.at[r], ep_rs.at[r], partner)

    e_send(0, 1, 0, 0, 128)
    e_send(0, 7, 1, 0, 128)
    e_share(0)
    pump(5)
    attend_far(3)
    for d in (1, 2):
        e_cps[d, 0].wait_recv()
        e_send(d, d + 1, 0, 0, 128)
        e_cps[8 - d, 1].wait_recv()
        e_send(8 - d, 7 - d, 1, 0, 128)
        e_share(d)
        e_share(8 - d)
    pump(6)
    e_cps[3, 0].wait_recv()
    e_send(3, 4, 0, 0, 64)
    e_cps[5, 1].wait_recv()
    e_send(5, 4, 1, 64, 128)
    e_share(3)
    e_share(5)
    attend_far(4)

    seen = pos_row[0:1, :] <= lax.broadcasted_iota(jnp.int32, (256, 256), 0) + e * 256

    @pl.loop(0, 4)
    def _(h):
        hs = pl.ds(pl.multiple_of(h * 128, 128), 128)
        scores = dot_nt(qry[:, hs], kp[:, hs].astype(BF))
        w = jnp.exp((scores - mrow[h][:, 0:1]) * INV_ROOT)
        wp[h] = jnp.where(seen, w, 0.0).astype(BF)

    e_cps[4, 0].wait_recv()
    e_cps[4, 1].wait_recv()
    e_share(4)
    for r in range(8):
        ep_cps[r].wait_recv()
    for g in range(2):
        for h in range(2):
            total = None
            for plane in range(4 * g, 4 * g + 4):
                term = e_buf[lax.rem(z - plane + 8, 8), h].astype(F32)
                total = term if total is None else total + term
            u_buf[128 * g : 128 * g + 128, 256 * h : 256 * h + 256] = total.astype(BF)

    hit = pos_row[0:1, :] == lax.broadcasted_iota(jnp.int32, (256, 256), 0) + e * 256
    scatter = jnp.where(hit, 1.0, 0.0).astype(BF)
    mixed_o[...] = (tok[...].astype(F32) + dot(scatter, u_buf[...])).astype(BF)

    @pl.loop(0, 4)
    def _(h):
        hs = pl.ds(pl.multiple_of(h * 128, 128), 128)
        num = acc[:, hs] + dot(wp[h], u_buf[:, hs])
        den = jnp.sum(lrow[h], axis=1, keepdims=True)
        att_o[:, hs] = (num / den).astype(BF)

    for cp in sent:
        cp.wait_send()
    w2_far.wait_send()


def body(tokens, queries, attn_keys, router, w_in, w_out, pick_rows, counts):
    rt = jnp.pad(router.T[:, None, :], ((0, 0), (0, 15), (0, 0)))
    vm = pl.BlockSpec(memory_space=pltpu.VMEM)
    sm = pl.BlockSpec(memory_space=pltpu.SMEM)
    hbm = pl.BlockSpec(memory_space=pl.ANY)
    V = pltpu.VMEM
    S = pltpu.SemaphoreType.DMA
    out = jax.ShapeDtypeStruct((256, 512), BF)
    return pl.pallas_call(
        kernel,
        name="layer",
        out_shape=(out, out),
        in_specs=[vm, vm, vm, vm, hbm, hbm, sm, sm],
        out_specs=(vm, vm),
        scratch_shapes=[
            V((2, 2, 48, 128), BF),
            V((16, 48, 128), BF),
            V((16, BLOCK_ROWS, 256), BF),
            V((2, 16, 256, 256), BF),
            V((2, 16, 256, 256), BF),
            V((128, 640), F32),
            V((128, 640), F32),
            V((128, 16), F32),
            V((128, 512), BF),
            V((128, 128), F32),
            V((4, 4, 128, 256), BF),
            V((4, 128, 256), F32),
            V((4, 2, 64, 256), BF),
            V((4, 2, 128, 256), BF),
            V((4, 128, 256), BF),
            V((2, 64, 256), BF),
            V((2, 128, 256), BF),
            V((8, 2, 128, 256), BF),
            V((256, 512), BF),
            V((8, 2, 256, 512), BF),
            V((8, 2, 256, 512), BF),
            V((256, 512), F32),
            V((4, 256, 128), F32),
            V((4, 256, 128), F32),
            V((256, 512), F32),
            V((4, 256, 256), BF),
            V((256, 128), jnp.int32),
            V((8, 256), jnp.int32),
            S((2,)),
            S((16,)), S((16,)),
            S((2,)), S((2,)),
            S((20,)), S((20,)),
            S((1,)), S((1,)),
            S((20,)), S((20,)),
            S((8, 2)), S((8, 2)),
            S((8,)), S((8,)),
            S((2, 8, 2)), S((2, 8, 2)),
            S((2, 8)), S((2, 8)),
        ],
        compiler_params=pltpu.CompilerParams(
            collective_id=0, has_side_effects=True, vmem_limit_bytes=50 * 2**20
        ),
    )(
        tokens, queries, attn_keys, rt,
        w_in.reshape(16, 2, 256, 256), w_out, pick_rows, counts,
    )


def solution(mesh):
    placed = (
        P("expert", "mp"),
        P("expert", "mp"),
        P("expert", "mp"),
        P("mp", None),
        P(None, ("expert", "mp")),
        P(("expert", "mp"), None),
        P(None, "expert", None),
        P(None, "expert"),
    )
    return jax.shard_map(
        body,
        mesh=mesh,
        in_specs=placed,
        out_specs=(P("expert", "mp"), P("expert", "mp")),
        check_vma=False,
    )
```

time: 300 us -> 84 us (0.28)
  waiting for transfers between devices: 168 us -> 0 us
  Pallas kernels: 0 us -> 76.8 us
  blocking collectives: 52.5 us -> 0 us
  matrix products: 25.9 us -> 0 us
  between operations: 15.7 us -> 0.65 us
  local copies, waits for them, and re-layouts: 18.2 us -> 6.37 us
  starting transfers between devices: 9.54 us -> 0 us
  other arithmetic: 9.33 us -> 0 us
    all_gather x3 -> x0, waiting for transfers between devices: 88.3 us -> none  [the longest x1 58.5 us: body(): lax.all_gather(picked_rows, 'mp', axis=1, tiled=True)]
    reduce_scatter x1 -> x0, waiting for transfers between devices: 79.9 us -> none  [body(): lax.psum_scatter(lax.dot_general(weight_part, hidden_t, (((0,), (0,)), ((...]
    pallas_call x0 -> x1, Pallas kernels: none -> 76.8 us  [body(): pl.pallas_call(kernel, name='layer', out_shape=(out, out), in_specs=[vm,...]
    psum x1 -> x0, blocking collectives: 30.9 us -> none  [body(): logits = lax.psum(partial_logits, 'mp')]
    dot_general x4 -> x0, matrix products: 25.9 us -> none  [the longest x1 11.2 us: body(): lax.dot_general(weight_part, hidden_t, (((0,), (0,)), ((), ())), preferre...]
    all_to_all x1 -> x0, blocking collectives: 21.6 us -> none  [body(): lax.all_to_all(outgoing, 'expert', split_axis=0, concat_axis=0, tiled=True)]
    all_to_all x1 -> x0, starting transfers between devices: 9.38 us -> none  [body(): lax.all_to_all(out_t.reshape(width_part, expert_devs, slot_count).astype(...]
    all_gather x1 -> x0, local copies, waits for them, and re-layouts: 6.48 us -> none  [body(): value_part = lax.all_gather(expert_mixed, 'expert', axis=0, tiled=True)]
  transfers between devices with their start and end apart: 5 -> 0, of which waited for: 3 -> 0; matrix products, arithmetic and copies ran while one was open for 5% -> 0% of each run, Pallas kernels for 0% -> 0%
where the time goes in v1:
time: 84 us; the launch traced here: 83.8 us
  Pallas kernels  76.8 us (91%)
  local copies, waits for them, and re-layouts  6.37 us (8%)
    pallas_call x1, Pallas kernels, body(): pl.pallas_call(kernel, name='layer', out_shape=(out, out), in_specs=[vm,...  76.8 us
    unnamed x11, local copies, waits for them, and re-layouts  5.67 us

profile of v1, /device:TPU:1, one launch (start us, length us, event | category | flops | bytes accessed | tf_op | source)
XLA Modules:
  0.0 83.8 jit_solution(11895327388378312315)
XLA Ops:
  0.6 0.7 copy.12.cnts
  1.4 0.7 copy.11
  2.1 0.0 copy-start
  2.1 0.9 %copy-done = bf16[256,512]{1,0:T(8,128)(2,1)S(1)} copy-done((bf16[256,512]{1,0:T(8,128)(2,1)S(1)}, bf16[256,512]{1,0:T(8,128)(2,1)}, u32[]{:S(2)}) %copy-start) | copy-done | bytes 262168
  3.0 0.0 copy-start.1
  3.0 0.9 %copy-done.1 = bf16[256,512]{1,0:T(8,128)(2,1)S(1)} copy-done((bf16[256,512]{1,0:T(8,128)(2,1)S(1)}, bf16[256,512]{1,0:T(8,128)(2,1)}, u32[]{:S(2)}) %copy-start.1) | copy-done | bytes 262168
  4.0 0.0 copy-start.2
  4.0 0.9 %copy-done.2 = bf16[256,512]{1,0:T(8,128)(2,1)S(1)} copy-done((bf16[256,512]{1,0:T(8,128)(2,1)S(1)}, bf16[256,512]{1,0:T(8,128)(2,1)}, u32[]{:S(2)}) %copy-start.2) | copy-done | bytes 262168
  4.9 0.0 copy-start.3
  4.9 0.7 copy-done.3
  5.6 76.8 %layer.1 = (bf16[256,512]{1,0:T(8,128)(2,1)S(1)}, bf16[256,512]{1,0:T(8,128)(2,1)S(1)}) custom-call(bf16[256,512]{1,0:T(8,128)(2,1)S(1)} %copy-done, bf16[256,512]{1,0:T(8,128)(2,1)S(1)} %copy-done.1, bf16[256,512]{1,0:T(8,128)(2,1)S(1)} %copy-done.2, bf16[2,16,512]{2,1,0:T(8,128)(2,1)S(1)} %pad.4.rt, bf16[16,2,256,256]{3,2,1,0:T(8,128)(2,1)} %bitcast.4, ...), custom_call_target="tpu_custom_call" | custom-call | tf_op jit(solution)/shard_map/layer/pallas_call | solution.py:495
  82.4 0.7 copy.15
  83.1 0.7 copy.16
  (1 shorter events, 0.0 us)
Async XLA Ops:
  2.1 1.0 %copy-start = (bf16[256,512]{1,0:T(8,128)(2,1)S(1)}, bf16[256,512]{1,0:T(8,128)(2,1)}, u32[]{:S(2)}) copy-start(bf16[256,512]{1,0:T(8,128)(2,1)} %tok.1) | copy-start | bytes 786436
  3.0 0.9 %copy-start.1 = (bf16[256,512]{1,0:T(8,128)(2,1)S(1)}, bf16[256,512]{1,0:T(8,128)(2,1)}, u32[]{:S(2)}) copy-start(bf16[256,512]{1,0:T(8,128)(2,1)} %qry.1) | copy-start | bytes 786436
  4.0 0.9 %copy-start.2 = (bf16[256,512]{1,0:T(8,128)(2,1)S(1)}, bf16[256,512]{1,0:T(8,128)(2,1)}, u32[]{:S(2)}) copy-start(bf16[256,512]{1,0:T(8,128)(2,1)} %key.1) | copy-start | bytes 786436
  4.9 0.7 copy-start.3

commit v2 on v1

--- a/solution.py
+++ b/solution.py
@@ -11,7 +11,7 @@
 F32 = jnp.float32
 NT = (((1,), (1,)), ((), ()))
 INV_ROOT = HEAD_DIM ** (-0.5)
-CUT, BLOCK_ROWS = 80, 144
+BLOCK_ROWS = 144
 
 
 def dot(a, b):
@@ -23,9 +23,10 @@
 
 
 def kernel(
-    tok, qry, key, rt, win, wout, picks, cnts, mixed_o, att_o,
+    tok_h, qry_h, key_h, rt, win, wout, picks, cnts, mixed_o, att_o,
+    tok, qry, key,
     a_msg, a_buf, xg, w1, w2, part, part_in, lgacc, hid, gate_s,
-    outb, t_own, rs_h, rs_f, t_sum, rp_h, rp_f, e_buf, u_buf,
+    outb, rs_in, t_sum, rp_in, f_sum, f_out, e_in, u_buf,
     kb, vb, acc, mrow, lrow, kp, wp, pos_col, pos_row,
     loc_sem, a_ss, a_rs, w_ss, w_rs, g_ss, g_rs, x_ss, x_rs,
     r_ss, r_rs, e_ss, e_rs, ep_ss, ep_rs, kv_ss, kv_rs, kvp_ss, kvp_rs,
@@ -68,6 +69,12 @@
         sent.append(cp)
         return cp
 
+    tok_in = pltpu.make_async_copy(tok_h, tok, loc_sem.at[2])
+    key_in = pltpu.make_async_copy(key_h, key, loc_sem.at[3])
+    qry_in = pltpu.make_async_copy(qry_h, qry, loc_sem.at[4])
+    tok_in.start()
+    key_in.start()
+    qry_in.start()
     w1_loc = pltpu.make_async_copy(win.at[:, c], w1.at[c], loc_sem.at[0])
     w1_loc.start()
     barrier = pltpu.get_barrier_semaphore()
@@ -75,7 +82,7 @@
         for dc in range(2):
             if dz or dc:
                 pl.semaphore_signal(barrier, inc=1, device_id=dev(dz, dc), device_id_type=MESH)
-    for d in (1, -1):
+    for d in (1, 2, 3):
         pl.semaphore_signal(barrier, inc=1, device_id=dev(dy=d), device_id_type=MESH)
         pl.semaphore_signal(barrier, inc=1, device_id=dev(dx=d), device_id_type=MESH)
 
@@ -84,17 +91,18 @@
     chosen = jnp.full((32, 256), -1, jnp.int32)
     row16 = lax.broadcasted_iota(jnp.int32, (16, 128), 0)
     lane16 = lax.broadcasted_iota(jnp.int32, (16, 128), 1)
-    meta = jnp.where(row16 == 0, cnts[0, 0], jnp.where(row16 == 1, cnts[1, 0], 0))
+    meta = jnp.where(row16 == 0, cnts[0, 0], jnp.where(row16 == 1, cnts[0, 1], 0))
     base = 16 * lax.rem(e, 8)
     for g in range(2):
         for j in range(16):
-            pick = picks[g, 0, j]
-            live = jnp.where(j < cnts[g, 0], pick, -1)
+            pick = picks[g, j]
+            live = jnp.where(j < cnts[0, g], pick, -1)
             chosen = jnp.where(row32 == 16 * g + j, live, chosen)
             meta = jnp.where(
                 (row16 == 2 + 2 * g + e // 8) & (lane16 == base + j), pick, meta
             )
     onehot = jnp.where(chosen == lane32, 1.0, 0.0).astype(BF)
+    tok_in.wait()
     rows = dot(onehot, tok[...]).astype(BF)
     meta_b = meta.astype(F32).astype(BF)
     for g in range(2):
@@ -103,7 +111,7 @@
             a_msg[g, h, 16:32, :] = rows[16 * g : 16 * g + 16, 256 * h + 128 : 256 * h + 256]
             a_msg[g, h, 32:48, :] = meta_b
     a_buf[e] = a_msg[group, c]
-    pl.semaphore_wait(barrier, 19)
+    pl.semaphore_wait(barrier, 21)
 
     a_cps = []
     for dz in (4, 3, 5, 2, 6, 1, 7, 0):
@@ -129,6 +137,8 @@
         src = buf.at[r, c] if src is None else src
         return send(src, buf.at[r, c], kvp_ss.at[which, r], kvp_rs.at[which, r], partner)
 
+    key_in.wait()
+    qry_in.wait()
     pieces = {}
     shared = {}
     pieces["k", 1] = kv_send(kb, 0, 0, 1, 0, key)
@@ -203,8 +213,8 @@
             hs = pl.ds(pl.multiple_of(h * 128, 128), 128)
             soft_step(h, dot_nt(qry[:, hs], kb[0, 0, :, hs]), vb[0, 0, :, hs])
 
-    def attend_chip(r):
-        @pl.loop(0, 4)
+    def attend_chip(r, first, last):
+        @pl.loop(first, last)
         def _(h):
             hs = pl.ds(pl.multiple_of(h * 128, 128), 128)
             k_h = kb[r, :, :, hs].reshape(512, 128)
@@ -217,18 +227,26 @@
         sel = jnp.where(pos_col[:, 0:1] == at, 1.0, 0.0).astype(BF)
         kp[...] += dot(sel, k_rows)
 
-    def attend_far(d):
-        for r, ok in ((d, z >= d), (8 - d, z >= 8 - d)):
+    def far_unit(d, side, part_no):
+        r, ok = ((d, z >= d), (8 - d, z >= 8 - d))[side]
+        if part_no == 0:
             for what in ("k", "v"):
                 shared[what, r].wait_recv()
 
-            @pl.when(ok)
-            def _():
-                attend_chip(r)
+        @pl.when(ok)
+        def _():
+            if part_no < 2:
+                attend_chip(r, 2 * part_no, 2 * part_no + 2)
+            else:
                 pick_keys((z - r) * 512, kb[r].reshape(512, 512))
 
-            if d == 4:
-                break
+    far = [(d, side, p) for d in (1, 2, 3) for side in (0, 1) for p in range(3)]
+    far += [(4, 0, p) for p in range(3)]
+
+    def fill(n):
+        for _ in range(n):
+            if far:
+                far_unit(*far.pop(0))
 
     attend_own()
     for what in ("k", "v"):
@@ -264,28 +282,26 @@
         got = a_buf[:, 16 * h : 16 * h + 16, :].reshape(256, 128)
         xg[m, 0:128, 128 * h : 128 * h + 128] = dot(mine, got).astype(BF)
     half_lanes = pl.ds(pl.multiple_of(256 * c, 256), 256)
-    xg[m, 128:144, :] = rt[group, :, half_lanes]
+    rt_row = jnp.where(group == 0, rt[0:1, half_lanes].astype(F32), rt[1:2, half_lanes].astype(F32))
+    xg[m, 128:144, :] = jnp.broadcast_to(rt_row, (16, 256)).astype(BF)
 
     g_cps = {}
 
-    def g_send(idx, b, lo, hi, to):
-        g_cps[idx] = send(
-            xg.at[b, pl.ds(lo, hi - lo)], xg.at[b, pl.ds(lo, hi - lo)],
-            g_ss.at[idx], g_rs.at[idx], to,
-        )
+    def g_send(idx, b, to):
+        g_cps[idx] = send(xg.at[b], xg.at[b], g_ss.at[idx], g_rs.at[idx], to)
 
     def g_second(i):
-        g_send(4 + 4 * i, blk(i, 0), 0, BLOCK_ROWS, sdev(1))
-        g_send(5 + 4 * i, blk(i, 0), 0, BLOCK_ROWS, sdev(-1))
-
-    def g_second_half(i):
-        g_cps[4 + 4 * i].wait_recv()
-        g_send(6 + 4 * i, blk(i, 3), 0, CUT, sdev(1))
-        g_cps[5 + 4 * i].wait_recv()
-        g_send(7 + 4 * i, blk(i, 1), CUT, BLOCK_ROWS, sdev(-1))
-
-    g_send(0, m, 0, BLOCK_ROWS, pdev(1))
-    g_send(1, m, 0, BLOCK_ROWS, pdev(-1))
+        for d in (2, 1, 3):
+            g_send(3 + 3 * i + d, blk(i, 0), sdev(d))
+
+    def g_wait(i, j):
+        if j:
+            g_cps[7 + 3 * i - j].wait_recv()
+        elif i:
+            g_cps[4 - i].wait_recv()
+
+    for d in (2, 1, 3):
+        g_send(d, m, pdev(d))
     g_second(0)
 
     at_lane = []
@@ -323,36 +339,21 @@
         part[:, 256:512] += dot(xb, w1[1, b])
         lgacc[...] += dot_nt(xb, xg[b, 128:144, :])
 
-    mm1(0, 0)
-    g_cps[0].wait_recv()
-    g_send(2, blk(3, 0), 0, CUT, pdev(1))
-    g_second(3)
-    g_cps[1].wait_recv()
-    g_send(3, blk(1, 0), CUT, BLOCK_ROWS, pdev(-1))
-    g_second(1)
-    mm1(3, 0)
-    mm1(1, 0)
-    g_second_half(0)
-    mm1(0, 3)
-    mm1(0, 1)
-    g_cps[2].wait_recv()
-    g_cps[3].wait_recv()
-    g_second(2)
-    mm1(2, 0)
+    for i in (3, 1, 2):
+        g_wait(i, 0)
+        g_second(i)
+    for i in (0, 3, 1, 2):
+        mm1(i, 0)
     pump(1)
-    for i in (3, 1, 2):
-        g_second_half(i)
-        mm1(i, 3)
-        mm1(i, 1)
-    attend_far(1)
-    pump(2)
     for i in (0, 3, 1, 2):
-        g_cps[6 + 4 * i].wait_recv()
-        g_cps[7 + 4 * i].wait_recv()
-        mm1(i, 2)
+        for j in (3, 1, 2):
+            g_wait(i, j)
+            mm1(i, j)
 
     part[:, 512:640] = jnp.broadcast_to(lgacc[:, 0:1], (128, 128))
     x_cp = send(part, part_in, x_ss.at[0], x_rs.at[0], partner)
+    pump(2)
+    fill(2)
     w2_loc.wait()
     w2_far.wait_recv()
     x_cp.wait_recv()
@@ -369,82 +370,60 @@
     def r_send(idx, src, dst, to):
         r_cps[idx] = send(src, dst, r_ss.at[idx], r_rs.at[idx], to)
 
-    order = (2, 3, 1, 0)
-    for i in order:
-        outb[i, 2] = mm2(i, 2).astype(BF)
-        r_send(4 * i, outb.at[i, 2, pl.ds(0, 64)], rs_h.at[i, 0], sdev(1))
-        r_send(4 * i + 1, outb.at[i, 2, pl.ds(64, 64)], rs_h.at[i, 1], sdev(-1))
-    for i in order:
-        o1 = mm2(i, 1)
-        o3 = mm2(i, 3)
-        r_cps[4 * i].wait_recv()
-        outb[i, 1, 0:64] = (o1[0:64] + rs_h[i, 0].astype(F32)).astype(BF)
-        outb[i, 1, 64:128] = o1[64:128].astype(BF)
-        r_send(4 * i + 2, outb.at[i, 1], rs_f.at[i, 0], sdev(1))
-        r_cps[4 * i + 1].wait_recv()
-        outb[i, 3, 0:64] = o3[0:64].astype(BF)
-        outb[i, 3, 64:128] = (o3[64:128] + rs_h[i, 1].astype(F32)).astype(BF)
-        r_send(4 * i + 3, outb.at[i, 3], rs_f.at[i, 1], sdev(-1))
-        t_own[i] = mm2(i, 0)
+    for i in (2, 3, 1, 0):
+        for j in (2, 3, 1):
+            outb[i, j] = mm2(i, j).astype(BF)
+            r_send(3 * i + j - 1, outb.at[i, j], rs_in.at[i, j - 1], sdev(j))
     pump(3)
 
     def t_of(i):
-        r_cps[4 * i + 2].wait_recv()
-        r_cps[4 * i + 3].wait_recv()
-        return t_own[i] + rs_f[i, 0].astype(F32) + rs_f[i, 1].astype(F32)
-
-    t_sum[2] = t_of(2).astype(BF)
-    r_send(16, t_sum.at[2, pl.ds(0, 64)], rp_h.at[0], pdev(1))
-    r_send(17, t_sum.at[2, pl.ds(64, 64)], rp_h.at[1], pdev(-1))
-    t3 = t_of(3)
-    t1 = t_of(1)
-    r_cps[17].wait_recv()
-    t_sum[3, 0:64] = t3[0:64].astype(BF)
-    t_sum[3, 64:128] = (t3[64:128] + rp_h[1].astype(F32)).astype(BF)
-    r_send(18, t_sum.at[3], rp_f.at[1], pdev(-1))
-    r_cps[16].wait_recv()
-    t_sum[1, 0:64] = (t1[0:64] + rp_h[0].astype(F32)).astype(BF)
-    t_sum[1, 64:128] = t1[64:128].astype(BF)
-    r_send(19, t_sum.at[1], rp_f.at[0], pdev(1))
-    attend_far(2)
+        total = mm2(i, 0)
+        for j in (3, 1, 2):
+            r_cps[3 * i + j - 1].wait_recv()
+            total = total + rs_in[i, j - 1].astype(F32)
+        return total
+
+    for i in (2, 3, 1):
+        t_sum[i] = t_of(i).astype(BF)
+        r_send(11 + i, t_sum.at[i], rp_in.at[i - 1], pdev(i))
+    full = t_of(0)
+    fill(4)
+    for i in (3, 1, 2):
+        r_cps[11 + i].wait_recv()
+        full = full + rp_in[i - 1].astype(F32)
+    f_sum[...] = full
+    f_out[...] = full.astype(BF)
+
+    zz = lax.rem(z, 4)
+    e_cps = []
+    for d in (2, 1, 3):
+        to_q = lax.rem(zz + d, 4)
+        e_cps.append(
+            send(
+                f_out.at[pl.ds(pl.multiple_of(32 * to_q, 32), 32)], e_in.at[d - 1],
+                e_ss.at[d - 1], e_rs.at[d - 1], ((4 * group + to_q) * 2 + c, m),
+            )
+        )
     pump(4)
-    t0 = t_of(0)
-    r_cps[18].wait_recv()
-    r_cps[19].wait_recv()
-    e_buf[0, c] = (t0 + rp_f[0].astype(F32) + rp_f[1].astype(F32)).astype(BF)
-
-    e_cps = {}
-    ep_cps = {}
-
-    def e_send(r_from, r_to, way, lo, hi):
-        e_cps[r_to, way] = send(
-            e_buf.at[r_from, c, pl.ds(lo, hi - lo)], e_buf.at[r_to, c, pl.ds(lo, hi - lo)],
-            e_ss.at[r_to, way], e_rs.at[r_to, way], dev(dz=1 if way == 0 else -1),
-        )
-
-    def e_share(r):
-        ep_cps[r] = send(e_buf.at[r, c], e_buf.at[r, c], ep_ss.at[r], ep_rs.at[r], partner)
-
-    e_send(0, 1, 0, 0, 128)
-    e_send(0, 7, 1, 0, 128)
-    e_share(0)
+    fill(2)
+    total = f_sum[pl.ds(pl.multiple_of(32 * zz, 32), 32), :]
+    for cp in e_cps:
+        cp.wait_recv()
+    for d in range(3):
+        total = total + e_in[d].astype(F32)
+    my_rows = pl.ds(pl.multiple_of(32 * z, 32), 32)
+    u_buf[c, my_rows, :] = total.astype(BF)
+    u_cps = []
+    for d in (4, 3, 5, 2, 6, 1, 7):
+        u_cps.append(
+            send(
+                u_buf.at[c, my_rows], u_buf.at[c, my_rows], e_ss.at[2 + d], e_rs.at[2 + d], dev(dz=d)
+            )
+        )
     pump(5)
-    attend_far(3)
-    for d in (1, 2):
-        e_cps[d, 0].wait_recv()
-        e_send(d, d + 1, 0, 0, 128)
-        e_cps[8 - d, 1].wait_recv()
-        e_send(8 - d, 7 - d, 1, 0, 128)
-        e_share(d)
-        e_share(8 - d)
+    fill(4)
     pump(6)
-    e_cps[3, 0].wait_recv()
-    e_send(3, 4, 0, 0, 64)
-    e_cps[5, 1].wait_recv()
-    e_send(5, 4, 1, 64, 128)
-    e_share(3)
-    e_share(5)
-    attend_far(4)
+    fill(len(far))
 
     seen = pos_row[0:1, :] <= lax.broadcasted_iota(jnp.int32, (256, 256), 0) + e * 256
 
@@ -455,50 +434,62 @@
         w = jnp.exp((scores - mrow[h][:, 0:1]) * INV_ROOT)
         wp[h] = jnp.where(seen, w, 0.0).astype(BF)
 
-    e_cps[4, 0].wait_recv()
-    e_cps[4, 1].wait_recv()
-    e_share(4)
-    for r in range(8):
-        ep_cps[r].wait_recv()
-    for g in range(2):
-        for h in range(2):
-            total = None
-            for plane in range(4 * g, 4 * g + 4):
-                term = e_buf[lax.rem(z - plane + 8, 8), h].astype(F32)
-                total = term if total is None else total + term
-            u_buf[128 * g : 128 * g + 128, 256 * h : 256 * h + 256] = total.astype(BF)
+    for cp in u_cps:
+        cp.wait_recv()
+    u_share = send(u_buf.at[c], u_buf.at[c], ep_ss.at[0], ep_rs.at[0], partner)
+    u_share.wait_recv()
 
     hit = pos_row[0:1, :] == lax.broadcasted_iota(jnp.int32, (256, 256), 0) + e * 256
     scatter = jnp.where(hit, 1.0, 0.0).astype(BF)
-    mixed_o[...] = (tok[...].astype(F32) + dot(scatter, u_buf[...])).astype(BF)
-
-    @pl.loop(0, 4)
-    def _(h):
-        hs = pl.ds(pl.multiple_of(h * 128, 128), 128)
-        num = acc[:, hs] + dot(wp[h], u_buf[:, hs])
+    for h in range(2):
+        cols = slice(256 * h, 256 * h + 256)
+        mixed_o[:, cols] = (tok[:, cols].astype(F32) + dot(scatter, u_buf[h])).astype(BF)
+    for h in range(4):
+        cols = slice(128 * h, 128 * h + 128)
+        u_h = u_buf[h // 2, :, 128 * (h % 2) : 128 * (h % 2) + 128]
+        num = acc[:, cols] + dot(wp[h], u_h)
         den = jnp.sum(lrow[h], axis=1, keepdims=True)
-        att_o[:, hs] = (num / den).astype(BF)
+        att_o[:, cols] = (num / den).astype(BF)
 
     for cp in sent:
         cp.wait_send()
     w2_far.wait_send()
 
 
+def hand_over(mixed, attended, mixed_o, att_o, buf, sem):
+    parts = [(a, b, i) for i in range(2) for a, b in ((mixed, mixed_o), (attended, att_o))]
+    ins, outs = [], []
+    for n, (a, b, i) in enumerate(parts):
+        rows = pl.ds(128 * i, 128)
+        ins.append(pltpu.make_async_copy(a.at[rows], buf.at[n], sem.at[n]))
+        outs.append(pltpu.make_async_copy(buf.at[n], b.at[rows], sem.at[4 + n]))
+    for cp in ins:
+        cp.start()
+    for i, cp in enumerate(ins):
+        cp.wait()
+        outs[i].start()
+    for cp in outs:
+        cp.wait()
+
+
 def body(tokens, queries, attn_keys, router, w_in, w_out, pick_rows, counts):
-    rt = jnp.pad(router.T[:, None, :], ((0, 0), (0, 15), (0, 0)))
+    rt = router.T
     vm = pl.BlockSpec(memory_space=pltpu.VMEM)
     sm = pl.BlockSpec(memory_space=pltpu.SMEM)
     hbm = pl.BlockSpec(memory_space=pl.ANY)
     V = pltpu.VMEM
     S = pltpu.SemaphoreType.DMA
     out = jax.ShapeDtypeStruct((256, 512), BF)
-    return pl.pallas_call(
+    mixed, attended = pl.pallas_call(
         kernel,
         name="layer",
         out_shape=(out, out),
-        in_specs=[vm, vm, vm, vm, hbm, hbm, sm, sm],
+        in_specs=[hbm, hbm, hbm, vm, hbm, hbm, sm, sm],
         out_specs=(vm, vm),
         scratch_shapes=[
+            V((256, 512), BF),
+            V((256, 512), BF),
+            V((256, 512), BF),
             V((2, 2, 48, 128), BF),
             V((16, 48, 128), BF),
             V((16, BLOCK_ROWS, 256), BF),
@@ -510,14 +501,13 @@
             V((128, 512), BF),
             V((128, 128), F32),
             V((4, 4, 128, 256), BF),
-            V((4, 128, 256), F32),
-            V((4, 2, 64, 256), BF),
-            V((4, 2, 128, 256), BF),
+            V((4, 3, 128, 256), BF),
             V((4, 128, 256), BF),
-            V((2, 64, 256), BF),
-            V((2, 128, 256), BF),
-            V((8, 2, 128, 256), BF),
-            V((256, 512), BF),
+            V((3, 128, 256), BF),
+            V((128, 256), F32),
+            V((128, 256), BF),
+            V((3, 32, 256), BF),
+            V((2, 256, 256), BF),
             V((8, 2, 256, 512), BF),
             V((8, 2, 256, 512), BF),
             V((256, 512), F32),
@@ -527,24 +517,32 @@
             V((4, 256, 256), BF),
             V((256, 128), jnp.int32),
             V((8, 256), jnp.int32),
-            S((2,)),
+            S((5,)),
             S((16,)), S((16,)),
             S((2,)), S((2,)),
-            S((20,)), S((20,)),
+            S((16,)), S((16,)),
             S((1,)), S((1,)),
-            S((20,)), S((20,)),
-            S((8, 2)), S((8, 2)),
-            S((8,)), S((8,)),
+            S((15,)), S((15,)),
+            S((10,)), S((10,)),
+            S((1,)), S((1,)),
             S((2, 8, 2)), S((2, 8, 2)),
             S((2, 8)), S((2, 8)),
         ],
         compiler_params=pltpu.CompilerParams(
-            collective_id=0, has_side_effects=True, vmem_limit_bytes=50 * 2**20
+            collective_id=0, has_side_effects=True, vmem_limit_bytes=58 * 2**20
         ),
     )(
         tokens, queries, attn_keys, rt,
-        w_in.reshape(16, 2, 256, 256), w_out, pick_rows, counts,
+        w_in.reshape(16, 2, 256, 256), w_out, pick_rows.reshape(2, 16), counts.reshape(1, 2),
     )
+    return pl.pallas_call(
+        hand_over,
+        name="hand_over",
+        out_shape=(out, out),
+        in_specs=[hbm, hbm],
+        out_specs=(hbm, hbm),
+        scratch_shapes=[V((4, 128, 512), BF), S((8,))],
+    )(mixed, attended)
 
 
 def solution(mesh):

time: 84 us -> 70.4 us (0.84)
  the two profiles are of different devices: /device:TPU:1 before, /device:TPU:225 now
where the time goes in v2:
time: 70.4 us; the launch traced here: 70.2 us
  Pallas kernels  69.6 us (99%)
    pallas_call x1, Pallas kernels, body(): pl.pallas_call(kernel, name='layer', out_shape=(out, out), in_specs=[hbm,...  67.8 us
    pallas_call x1, Pallas kernels, body(): pl.pallas_call(hand_over, name='hand_over', out_shape=(out, out), in_spec...  1.82 us

profile of v2, /device:TPU:225, one launch (start us, length us, event | category | flops | bytes accessed | tf_op | source)
XLA Modules:
  0.0 70.2 jit_solution(11586894383257325774)
XLA Ops:
  0.6 67.8 %layer.1 = (bf16[256,512]{1,0:T(8,128)(2,1)}, bf16[256,512]{1,0:T(8,128)(2,1)}) custom-call(bf16[256,512]{1,0:T(8,128)(2,1)} %tok_h.1, bf16[256,512]{1,0:T(8,128)(2,1)} %qry_h.1, bf16[256,512]{1,0:T(8,128)(2,1)} %key_h.1, bf16[2,512]{1,0:T(2,128)(2,1)} %bitcast.5, bf16[16,2,256,256]{3,2,1,0:T(8,128)(2,1)} %bitcast.4, bf16[256,8192]{1,0:T(8,128)(2,1)} %wout.1, ...), custom_call_target="tpu_custom_call" | custom-call | tf_op jit(solution)/shard_map/layer/pallas_call | solution.py:483
  68.4 1.8 %hand_over.1 = (bf16[256,512]{1,0:T(8,128)(2,1)}, bf16[256,512]{1,0:T(8,128)(2,1)}) custom-call(bf16[256,512]{1,0:T(8,128)(2,1)} %get-tuple-element.4.mixed, bf16[256,512]{1,0:T(8,128)(2,1)} %get-tuple-element.5.attended), custom_call_target="tpu_custom_call" | custom-call | tf_op jit(solution)/shard_map/hand_over/pallas_call | solution.py:538

commit v3 on v2

--- a/solution.py
+++ b/solution.py
@@ -10,7 +10,7 @@
 BF = jnp.bfloat16
 F32 = jnp.float32
 NT = (((1,), (1,)), ((), ()))
-INV_ROOT = HEAD_DIM ** (-0.5)
+INV_ROOT = HEAD_DIM ** (-0.5) * 1.4426950408889634
 BLOCK_ROWS = 144
 
 
@@ -183,8 +183,8 @@
         hs = pl.ds(pl.multiple_of(h * 128, 128), 128)
         old = mrow[h][:, 0:1]
         new = jnp.maximum(old, jnp.max(scores, axis=1, keepdims=True))
-        alpha = jnp.exp((old - new) * INV_ROOT)
-        w = jnp.exp((scores - new) * INV_ROOT)
+        alpha = jnp.exp2((old - new) * INV_ROOT)
+        w = jnp.exp2((scores - new) * INV_ROOT)
         total = w[:, 0:128]
         for i in range(1, scores.shape[1] // 128):
             total = total + w[:, 128 * i : 128 * i + 128]
@@ -202,7 +202,7 @@
             hs = pl.ds(pl.multiple_of(h * 128, 128), 128)
             scores = jnp.where(allowed, dot_nt(qry[:, hs], key[:, hs]), -1e30)
             new = jnp.max(scores, axis=1, keepdims=True)
-            w = jnp.exp((scores - new) * INV_ROOT)
+            w = jnp.exp2((scores - new) * INV_ROOT)
             lrow[h] = w[:, 0:128] + w[:, 128:256]
             acc[:, hs] = dot(w.astype(BF), tok[:, hs])
             mrow[h] = jnp.broadcast_to(new, (256, 128))
@@ -241,7 +241,6 @@
                 pick_keys((z - r) * 512, kb[r].reshape(512, 512))
 
     far = [(d, side, p) for d in (1, 2, 3) for side in (0, 1) for p in range(3)]
-    far += [(4, 0, p) for p in range(3)]
 
     def fill(n):
         for _ in range(n):
@@ -326,7 +325,6 @@
     def _():
         pick_keys(z * 512, kb[0, 0])
 
-    pump(0)
     part[...] = jnp.zeros((128, 640), F32)
     lgacc[...] = jnp.zeros((128, 16), F32)
     w1_loc.wait()
@@ -344,16 +342,19 @@
         g_second(i)
     for i in (0, 3, 1, 2):
         mm1(i, 0)
-    pump(1)
+    pump(0)
     for i in (0, 3, 1, 2):
         for j in (3, 1, 2):
             g_wait(i, j)
             mm1(i, j)
+        if i == 3:
+            pump(1)
 
     part[:, 512:640] = jnp.broadcast_to(lgacc[:, 0:1], (128, 128))
     x_cp = send(part, part_in, x_ss.at[0], x_rs.at[0], partner)
+    fill(2)
     pump(2)
-    fill(2)
+    fill(1)
     w2_loc.wait()
     w2_far.wait_recv()
     x_cp.wait_recv()
@@ -375,6 +376,7 @@
             outb[i, j] = mm2(i, j).astype(BF)
             r_send(3 * i + j - 1, outb.at[i, j], rs_in.at[i, j - 1], sdev(j))
     pump(3)
+    fill(3)
 
     def t_of(i):
         total = mm2(i, 0)
@@ -421,9 +423,27 @@
             )
         )
     pump(5)
-    fill(4)
+    fill(3)
     pump(6)
     fill(len(far))
+
+    def attend_opposite(core):
+        @pl.when(z >= 4)
+        def _():
+            @pl.loop(0, 4)
+            def _(h):
+                hs = pl.ds(pl.multiple_of(h * 128, 128), 128)
+                soft_step(h, dot_nt(qry[:, hs], kb[4, core, :, hs]), vb[4, core, :, hs])
+
+    attend_opposite(c)
+    shared["k", 4].wait_recv()
+    shared["v", 4].wait_recv()
+    attend_opposite(oc)
+
+    @pl.when(z >= 4)
+    def _():
+        pick_keys((z - 4) * 512, kb[4].reshape(512, 512))
+
 
     seen = pos_row[0:1, :] <= lax.broadcasted_iota(jnp.int32, (256, 256), 0) + e * 256
 
@@ -431,7 +451,7 @@
     def _(h):
         hs = pl.ds(pl.multiple_of(h * 128, 128), 128)
         scores = dot_nt(qry[:, hs], kp[:, hs].astype(BF))
-        w = jnp.exp((scores - mrow[h][:, 0:1]) * INV_ROOT)
+        w = jnp.exp2((scores - mrow[h][:, 0:1]) * INV_ROOT)
         wp[h] = jnp.where(seen, w, 0.0).astype(BF)
 
     for cp in u_cps:

time: 70.4 us -> 67.9 us (0.964)
  the two profiles are of different devices: /device:TPU:225 before, /device:TPU:1 now
where the time goes in v3:
time: 67.9 us; the launch traced here: 66.7 us
  Pallas kernels  66.1 us (97%)
    pallas_call x1, Pallas kernels, body(): pl.pallas_call(kernel, name='layer', out_shape=(out, out), in_specs=[hbm,...  64.2 us
    pallas_call x1, Pallas kernels, body(): pl.pallas_call(hand_over, name='hand_over', out_shape=(out, out), in_spec...  1.82 us

profile of v3, /device:TPU:1, one launch (start us, length us, event | category | flops | bytes accessed | tf_op | source)
XLA Modules:
  0.0 66.7 jit_solution(12850944294246864213)
XLA Ops:
  0.6 64.2 %layer.1 = (bf16[256,512]{1,0:T(8,128)(2,1)}, bf16[256,512]{1,0:T(8,128)(2,1)}) custom-call(bf16[256,512]{1,0:T(8,128)(2,1)} %tok_h.1, bf16[256,512]{1,0:T(8,128)(2,1)} %qry_h.1, bf16[256,512]{1,0:T(8,128)(2,1)} %key_h.1, bf16[2,512]{1,0:T(2,128)(2,1)} %bitcast.5, bf16[16,2,256,256]{3,2,1,0:T(8,128)(2,1)} %bitcast.4, bf16[256,8192]{1,0:T(8,128)(2,1)} %wout.1, ...), custom_call_target="tpu_custom_call" | custom-call | tf_op jit(solution)/shard_map/layer/pallas_call | solution.py:503
  64.9 1.8 %hand_over.1 = (bf16[256,512]{1,0:T(8,128)(2,1)}, bf16[256,512]{1,0:T(8,128)(2,1)}) custom-call(bf16[256,512]{1,0:T(8,128)(2,1)} %get-tuple-element.4.mixed, bf16[256,512]{1,0:T(8,128)(2,1)} %get-tuple-element.5.attended), custom_call_target="tpu_custom_call" | custom-call | tf_op jit(solution)/shard_map/hand_over/pallas_call | solution.py:558

commit v4 on v3

--- a/solution.py
+++ b/solution.py
@@ -423,7 +423,7 @@
             )
         )
     pump(5)
-    fill(3)
+    fill(5)
     pump(6)
     fill(len(far))
 

time: 67.9 us -> 67.3 us (level)
  no operation moved by 1% of the time
where the time goes in v4:
time: 67.3 us; the launch traced here: 66.7 us
  Pallas kernels  66.1 us (98%)
    pallas_call x1, Pallas kernels, body(): pl.pallas_call(kernel, name='layer', out_shape=(out, out), in_specs=[hbm,...  64.2 us
    pallas_call x1, Pallas kernels, body(): pl.pallas_call(hand_over, name='hand_over', out_shape=(out, out), in_spec...  1.82 us

profile of v4, /device:TPU:1, one launch (start us, length us, event | category | flops | bytes accessed | tf_op | source)
XLA Modules:
  0.0 66.7 jit_solution(14544917428398518082)
XLA Ops:
  0.6 64.2 %layer.1 = (bf16[256,512]{1,0:T(8,128)(2,1)}, bf16[256,512]{1,0:T(8,128)(2,1)}) custom-call(bf16[256,512]{1,0:T(8,128)(2,1)} %tok_h.1, bf16[256,512]{1,0:T(8,128)(2,1)} %qry_h.1, bf16[256,512]{1,0:T(8,128)(2,1)} %key_h.1, bf16[2,512]{1,0:T(2,128)(2,1)} %bitcast.5, bf16[16,2,256,256]{3,2,1,0:T(8,128)(2,1)} %bitcast.4, bf16[256,8192]{1,0:T(8,128)(2,1)} %wout.1, ...), custom_call_target="tpu_custom_call" | custom-call | tf_op jit(solution)/shard_map/layer/pallas_call | solution.py:503
  64.9 1.8 %hand_over.1 = (bf16[256,512]{1,0:T(8,128)(2,1)}, bf16[256,512]{1,0:T(8,128)(2,1)}) custom-call(bf16[256,512]{1,0:T(8,128)(2,1)} %get-tuple-element.4.mixed, bf16[256,512]{1,0:T(8,128)(2,1)} %get-tuple-element.5.attended), custom_call_target="tpu_custom_call" | custom-call | tf_op jit(solution)/shard_map/hand_over/pallas_call | solution.py:558

commit v5 on v4

--- a/solution.py
+++ b/solution.py
@@ -435,6 +435,9 @@
                 hs = pl.ds(pl.multiple_of(h * 128, 128), 128)
                 soft_step(h, dot_nt(qry[:, hs], kb[4, core, :, hs]), vb[4, core, :, hs])
 
+    for cp in u_cps:
+        cp.wait_recv()
+    u_share = send(u_buf.at[c], u_buf.at[c], ep_ss.at[0], ep_rs.at[0], partner)
     attend_opposite(c)
     shared["k", 4].wait_recv()
     shared["v", 4].wait_recv()
@@ -454,9 +457,6 @@
         w = jnp.exp2((scores - mrow[h][:, 0:1]) * INV_ROOT)
         wp[h] = jnp.where(seen, w, 0.0).astype(BF)
 
-    for cp in u_cps:
-        cp.wait_recv()
-    u_share = send(u_buf.at[c], u_buf.at[c], ep_ss.at[0], ep_rs.at[0], partner)
     u_share.wait_recv()
 
     hit = pos_row[0:1, :] == lax.broadcasted_iota(jnp.int32, (256, 256), 0) + e * 256

time: 67.3 us -> 66.8 us (level)
  no operation moved by 1% of the time
where the time goes in v5:
time: 66.8 us; the launch traced here: 66.7 us
  Pallas kernels  66.1 us (99%)
    pallas_call x1, Pallas kernels, body(): pl.pallas_call(kernel, name='layer', out_shape=(out, out), in_specs=[hbm,...  64.2 us
    pallas_call x1, Pallas kernels, body(): pl.pallas_call(hand_over, name='hand_over', out_shape=(out, out), in_spec...  1.82 us

profile of v5, /device:TPU:1, one launch (start us, length us, event | category | flops | bytes accessed | tf_op | source)
XLA Modules:
  0.0 66.7 jit_solution(8249867451728075540)
XLA Ops:
  0.6 64.2 %layer.1 = (bf16[256,512]{1,0:T(8,128)(2,1)}, bf16[256,512]{1,0:T(8,128)(2,1)}) custom-call(bf16[256,512]{1,0:T(8,128)(2,1)} %tok_h.1, bf16[256,512]{1,0:T(8,128)(2,1)} %qry_h.1, bf16[256,512]{1,0:T(8,128)(2,1)} %key_h.1, bf16[2,512]{1,0:T(2,128)(2,1)} %bitcast.5, bf16[16,2,256,256]{3,2,1,0:T(8,128)(2,1)} %bitcast.4, bf16[256,8192]{1,0:T(8,128)(2,1)} %wout.1, ...), custom_call_target="tpu_custom_call" | custom-call | tf_op jit(solution)/shard_map/layer/pallas_call | solution.py:503
  64.9 1.8 %hand_over.1 = (bf16[256,512]{1,0:T(8,128)(2,1)}, bf16[256,512]{1,0:T(8,128)(2,1)}) custom-call(bf16[256,512]{1,0:T(8,128)(2,1)} %get-tuple-element.4.mixed, bf16[256,512]{1,0:T(8,128)(2,1)} %get-tuple-element.5.attended), custom_call_target="tpu_custom_call" | custom-call | tf_op jit(solution)/shard_map/hand_over/pallas_call | solution.py:558
